TPU v7x, 512 devices: a whole 4x8x8 slice. The times are simulated.
512 devices in a mesh: band: 128 (over z, y_lo, x, core), head: 4 (over y_hi).
Axes of the slice: x: 4, y: 8 (y_hi: 4, y_lo: 2; y = y_hi * 2 + y_lo), z: 8, core: 2. Of those that a mesh axis runs over, the one named last changes fastest.
Arguments:
- queries: bfloat16 [16384, 1536], P('band', 'head'), as said below
- keys: bfloat16 [16384, 1536], P('band', 'head'), as said below
- values: bfloat16 [16384, 1536], P('band', 'head'), may hold values from -6 to 6
- d_out: bfloat16 [16384, 1536], P('band', 'head'), may hold values from -6 to 6
- gain: float32 [1536], P('head'), may hold values from 0.1 to 1.9
- blocks_on: int32 [128, 4], P('band'), may hold values 0 or 1
Outputs:
- out: bfloat16 [16384, 1536], P('band', 'head')
- d_queries: bfloat16 [16384, 1536], P('band', 'head')
- d_keys: bfloat16 [16384, 1536], P('band', 'head')
- d_values: bfloat16 [16384, 1536], P('band', 'head')
Inputs may be any that keep to these rules, and one draw needn't show every extreme that they name: `queries`: entries lie within -180 to 180. `keys`: entries lie within -6 to 6.
All inputs are finite; a program needn't handle non-finite values. No bound on the sum of `blocks_on` on one device may be relied on, other than what follows from the above.
Results may differ from a plain program's by a relative error of at most 0.0063.
Values may be sent and summed in bfloat16 or wider, within the bound.
A program may use at most 64 MiB of HBM per device.

v0:
```python
import jax
import jax.numpy as jnp
from jax import lax
from jax.sharding import PartitionSpec as P

HEAD_DIM = 128
NEG = -1e30
EPS = 1e-06


def from_behind(array, axis, by):
    devices = lax.axis_size(axis)
    pairs = [(i, i + by) for i in range(devices) if 0 <= i + by < devices]
    return lax.ppermute(array, axis, pairs)


def row_pairs_matrix(left, right):
    return lax.dot_general(
        left, right, (((1,), (1,)), ((), ())), preferred_element_type=jnp.float32
    )


def cols_by_cols(left, right):
    return lax.dot_general(
        left, right, (((0,), (0,)), ((), ())), preferred_element_type=jnp.float32
    )


def product(left, right):
    return jnp.dot(left, right, preferred_element_type=jnp.float32)


def one_head(matrix, head_index):
    return matrix[:, head_index * HEAD_DIM : (head_index + 1) * HEAD_DIM]


def local(queries, keys, values, d_out, gain, blocks_on):
    row_count = queries.shape[0]
    heads_here = queries.shape[1] // HEAD_DIM
    blocks = lax.axis_size("band")
    spacing = blocks // 8
    block_offsets = [-2 * spacing, -spacing, spacing, 2 * spacing]
    position = lax.axis_index("band")
    scaling = HEAD_DIM ** (-0.5)
    full_width = queries.shape[1] * lax.axis_size("head")
    key_value = jnp.stack([keys, values])
    reached = [key_value]
    allowed = [jnp.ones((), jnp.bool_)]
    for slot_index, offset in enumerate(block_offsets):
        reached.append(from_behind(key_value, "band", -offset))
        target = position + offset
        allowed.append((target >= 0) & (target < blocks) & (blocks_on[0, slot_index] == 1))
    gathered = jnp.concatenate(reached, axis=1)
    key_all = gathered[0]
    value_all = gathered[1]
    column_ok = jnp.repeat(jnp.stack(allowed), row_count)

    def scores(head_index):
        raw_score = (
            row_pairs_matrix(one_head(queries, head_index), one_head(key_all, head_index)) * scaling
        )
        return jnp.where(column_ok[None, :], raw_score, NEG)

    peaks, totals, pieces = ([], [], [])
    for head_index in range(heads_here):
        score = scores(head_index)
        peak = jnp.max(score, axis=1)
        exponent = jnp.exp(score - peak[:, None])
        total = jnp.sum(exponent, axis=1)
        weight_probs = (exponent / total[:, None]).astype(jnp.bfloat16)
        pieces.append(product(weight_probs, one_head(value_all, head_index)).astype(jnp.bfloat16))
        peaks.append(peak)
        totals.append(total)
    attention = jnp.concatenate(pieces, axis=1)
    attention_wide = attention.astype(jnp.float32)
    square_sum = lax.psum(jnp.sum(attention_wide * attention_wide, axis=1), "head")
    inverse = lax.rsqrt(square_sum / full_width + EPS)
    out = (attention_wide * inverse[:, None] * gain).astype(jnp.bfloat16)
    gradient_pass = d_out.astype(jnp.float32) * gain
    along = lax.psum(jnp.sum(gradient_pass * attention_wide, axis=1), "head")
    d_attn = (
        inverse[:, None] * gradient_pass
        - attention_wide * (inverse**3 * along / full_width)[:, None]
    ).astype(jnp.bfloat16)
    deltas = [
        jnp.sum(
            one_head(d_attn, head_index).astype(jnp.float32) * one_head(attention_wide, head_index),
            axis=1,
        )
        for head_index in range(heads_here)
    ]
    query_parts, key_parts, value_parts = ([], [], [])
    for head_index in range(heads_here):
        score = scores(head_index)
        probs = jnp.exp(score - peaks[head_index][:, None]) / totals[head_index][:, None]
        upstream = one_head(d_attn, head_index)
        d_weights = row_pairs_matrix(upstream, one_head(value_all, head_index))
        d_score = (probs * (d_weights - deltas[head_index][:, None])).astype(jnp.bfloat16)
        query_parts.append(product(d_score, one_head(key_all, head_index)) * scaling)
        weight_probs = probs.astype(jnp.bfloat16)
        key_parts.append(cols_by_cols(d_score, one_head(queries, head_index)) * scaling)
        value_parts.append(cols_by_cols(weight_probs, upstream))
    d_queries = jnp.concatenate(query_parts, axis=1).astype(jnp.bfloat16)
    stacked_grads = jnp.stack(
        [jnp.concatenate(key_parts, axis=1), jnp.concatenate(value_parts, axis=1)]
    )
    summed = stacked_grads[:, :row_count]
    for slot_index, offset in enumerate(block_offsets):
        outgoing = stacked_grads[
            :, (slot_index + 1) * row_count : (slot_index + 2) * row_count
        ].astype(jnp.bfloat16)
        arrived = from_behind(outgoing, "band", offset)
        summed = summed + arrived.astype(jnp.float32)
    d_keys = summed[0].astype(jnp.bfloat16)
    d_values = summed[1].astype(jnp.bfloat16)
    return (out, d_queries, d_keys, d_values)


def solution(mesh):
    in_specs = (
        P("band", "head"),
        P("band", "head"),
        P("band", "head"),
        P("band", "head"),
        P("head"),
        P("band", None),
    )
    out_specs = (P("band", "head"), P("band", "head"), P("band", "head"), P("band", "head"))
    return jax.shard_map(local, mesh=mesh, in_specs=in_specs, out_specs=out_specs, check_vma=False)
```

profile of v0, /device:TPU:6, one launch (start us, length us, event | category | flops | bytes accessed | tf_op | source)
XLA Modules:
  0.0 70.1 jit_solution(15155738258795446889)
XLA Ops:
  0.6 1.0 %pad_maximum_fusion.1 = (bf16[2,128,384]{2,1,0:T(8,128)(2,1)S(1)}, bf16[2,640,384]{2,1,0:T(8,128)(2,1)S(1)}) fusion(bf16[1,128,384]{2,1,0:T(8,128)(2,1)} %bitcast.45, bf16[1,128,384]{2,1,0:T(8,128)(2,1)} %bitcast.46), kind=kLoop, calls=%fused_computation.53 | loop fusion | flops 393215 | bytes 589824 | tf_op jit(solution)/shard_map/stack | solution.py:46
  1.6 1.3 %collective-permute-start.2 = (bf16[2,128,384]{2,1,0:T(8,128)(2,1)S(1)}, bf16[2,128,384]{2,1,0:T(8,128)(2,1)S(1)}, u32[]{:S(2)}, u32[]{:S(2)}) collective-permute-start(bf16[2,128,384]{2,1,0:T(8,128)(2,1)S(1)} %get-tuple-element.23), channel_id=1, source_target_pairs={{64,0},{68,4},{72,8},{76,12},{80,16},{84,20},{88,24},{92,28},{96,3... | collective-permute-start | bytes 589832 | tf_op jit(solution)/shard_map/ppermute | solution.py:14
  2.9 4.9 %collective-permute-start.1 = (bf16[2,128,384]{2,1,0:T(8,128)(2,1)S(1)}, bf16[2,128,384]{2,1,0:T(8,128)(2,1)S(1)}, u32[]{:S(2)}, u32[]{:S(2)}) collective-permute-start(bf16[2,128,384]{2,1,0:T(8,128)(2,1)S(1)} %get-tuple-element.23), channel_id=1, source_target_pairs={{0,64},{4,68},{8,72},{12,76},{16,80},{20,84},{24,88},{28,92},{32,9... | collective-permute-start | bytes 589832 | tf_op jit(solution)/shard_map/ppermute | solution.py:14
  7.8 6.1 %collective-permute-start = (bf16[2,128,384]{2,1,0:T(8,128)(2,1)S(1)}, bf16[2,128,384]{2,1,0:T(8,128)(2,1)S(1)}, u32[]{:S(2)}, u32[]{:S(2)}) collective-permute-start(bf16[2,128,384]{2,1,0:T(8,128)(2,1)S(1)} %get-tuple-element.23), channel_id=1, source_target_pairs={{0,128},{4,132},{8,136},{12,140},{16,144},{20,148},{24,152},{28,15... | collective-permute-start | bytes 589832 | tf_op jit(solution)/shard_map/ppermute | solution.py:14
  13.9 1.3 %collective-permute-start.3 = (bf16[2,128,384]{2,1,0:T(8,128)(2,1)S(1)}, bf16[2,128,384]{2,1,0:T(8,128)(2,1)S(1)}, u32[]{:S(2)}, u32[]{:S(2)}) collective-permute-start(bf16[2,128,384]{2,1,0:T(8,128)(2,1)S(1)} %get-tuple-element.23), channel_id=1, source_target_pairs={{128,0},{132,4},{136,8},{140,12},{144,16},{148,20},{152,24},{156,2... | collective-permute-start | bytes 589832 | tf_op jit(solution)/shard_map/ppermute | solution.py:14
  15.2 1.4 %fusion.59 = (s32[1,1]{1,0:T(1,128)}, s32[1,1]{1,0:T(1,128)}, s32[1,1]{1,0:T(1,128)}, s32[1,1]{1,0:T(1,128)}) fusion(s32[1,4]{1,0:T(1,128)} %param.11), kind=kLoop, calls=%fused_computation.108 | loop fusion | bytes 32 | tf_op jit(solution)/shard_map/slice | solution.py:52
  19.5 1.0 %copy.10 = bf16[128,384]{0,1:T(8,128)(2,1)S(1)} copy(bf16[128,384]{1,0:T(8,128)(2,1)} %param.9) | data formatting | bytes 196608 | tf_op args[3]
  20.6 8.5 %collective-permute-done.3 = bf16[2,128,384]{2,1,0:T(8,128)(2,1)S(1)} collective-permute-done((bf16[2,128,384]{2,1,0:T(8,128)(2,1)S(1)}, bf16[2,128,384]{2,1,0:T(8,128)(2,1)S(1)}, u32[]{:S(2)}, u32[]{:S(2)}) %collective-permute-start.3) | collective-permute-done | bytes 196640 | tf_op jit(solution)/shard_map/ppermute | solution.py:14
  29.3 0.8 %copy-done = bf16[128,384]{1,0:T(8,128)(2,1)S(1)} copy-done((bf16[128,384]{1,0:T(8,128)(2,1)S(1)}, bf16[128,384]{1,0:T(8,128)(2,1)}, u32[]{:S(2)}) %copy-start) | copy-done | bytes 98328
  30.3 0.3 fusion.61
  32.4 12.9 %all-reduce = (f32[128]{0:T(128)S(1)}, f32[128]{0:T(128)S(1)}) all-reduce(f32[128]{0:T(128)S(1)} %get-tuple-element.12, f32[128]{0:T(128)S(1)} %get-tuple-element.11), channel_id=1, replica_groups=mesh['band'=128,'head'=4] {'head'}, use_global_device_ids=true, to_apply=%region_7.8 | all-reduce | flops 256 | bytes 2048 | tf_op jit(solution)/shard_map/psum | solution.py:76
  45.7 0.3 fusion.11
  46.3 0.3 fusion.10
  48.1 0.8 %fusion.58 = (bf16[2,128,384]{2,1,0:T(8,128)(2,1)}, bf16[2,128,384]{2,1,0:T(8,128)(2,1)}, bf16[2,128,384]{2,1,0:T(8,128)(2,1)S(1)}, bf16[2,128,384]{2,1,0:T(8,128)(2,1)S(1)}) fusion(bf16[2,640,384]{2,1,0:T(8,128)(2,1)S(1)} %fusion), kind=kLoop, calls=%fused_computation.107 | loop fusion | bytes 1572864 | tf_op jit(solution)/shard_map/slice | solution.py:109
  48.9 1.3 %collective-permute-start.4 = (bf16[2,128,384]{2,1,0:T(8,128)(2,1)}, bf16[2,128,384]{2,1,0:T(8,128)(2,1)S(1)}, u32[]{:S(2)}, u32[]{:S(2)}) collective-permute-start(bf16[2,128,384]{2,1,0:T(8,128)(2,1)} %get-tuple-element.15), channel_id=1, source_target_pairs={{128,0},{132,4},{136,8},{140,12},{144,16},{148,20},{152,24},{156,2... | collective-permute-start | bytes 589832 | tf_op jit(solution)/shard_map/ppermute | solution.py:14
  50.2 5.5 %collective-permute-start.7 = (bf16[2,128,384]{2,1,0:T(8,128)(2,1)}, bf16[2,128,384]{2,1,0:T(8,128)(2,1)S(1)}, u32[]{:S(2)}, u32[]{:S(2)}) collective-permute-start(bf16[2,128,384]{2,1,0:T(8,128)(2,1)} %get-tuple-element.16), channel_id=1, source_target_pairs={{0,128},{4,132},{8,136},{12,140},{16,144},{20,148},{24,152},{28,15... | collective-permute-start | bytes 589832 | tf_op jit(solution)/shard_map/ppermute | solution.py:14
  55.7 5.0 %collective-permute-start.6 = (bf16[2,128,384]{2,1,0:T(8,128)(2,1)S(1)}, bf16[2,128,384]{2,1,0:T(8,128)(2,1)}, u32[]{:S(2)}, u32[]{:S(2)}) collective-permute-start(bf16[2,128,384]{2,1,0:T(8,128)(2,1)S(1)} %get-tuple-element.17), channel_id=1, source_target_pairs={{0,64},{4,68},{8,72},{12,76},{16,80},{20,84},{24,88},{28,92},{32,9... | collective-permute-start | bytes 589832 | tf_op jit(solution)/shard_map/ppermute | solution.py:14
  60.6 1.3 %collective-permute-start.5 = (bf16[2,128,384]{2,1,0:T(8,128)(2,1)S(1)}, bf16[2,128,384]{2,1,0:T(8,128)(2,1)}, u32[]{:S(2)}, u32[]{:S(2)}) collective-permute-start(bf16[2,128,384]{2,1,0:T(8,128)(2,1)S(1)} %get-tuple-element.18), channel_id=1, source_target_pairs={{64,0},{68,4},{72,8},{76,12},{80,16},{84,20},{88,24},{92,28},{96,3... | collective-permute-start | bytes 589832 | tf_op jit(solution)/shard_map/ppermute | solution.py:14
  61.9 0.3 fusion.12
  62.2 0.8 %copy.20 = bf16[128,384]{1,0:T(8,128)(2,1)} copy(bf16[128,384]{0,1:T(8,128)(2,1)S(1)} %get-tuple-element.26) | data formatting | bytes 196608
  63.0 0.8 %copy.21 = bf16[128,384]{1,0:T(8,128)(2,1)} copy(bf16[128,384]{0,1:T(8,128)(2,1)S(1)} %pad_maximum_fusion.3) | data formatting | bytes 196608
  63.7 4.6 %collective-permute-done.5 = bf16[2,128,384]{2,1,0:T(8,128)(2,1)} collective-permute-done((bf16[2,128,384]{2,1,0:T(8,128)(2,1)S(1)}, bf16[2,128,384]{2,1,0:T(8,128)(2,1)}, u32[]{:S(2)}, u32[]{:S(2)}) %collective-permute-start.5) | collective-permute-done | bytes 196640 | tf_op jit(solution)/shard_map/ppermute | solution.py:14
  68.3 1.1 %fusion.18 = bf16[2,128,384]{2,1,0:T(8,128)(2,1)S(1)} fusion(f32[1,640,384]{2,1,0:T(8,128)S(1)} %get-tuple-element.39, f32[1,640,384]{2,1,0:T(8,128)S(1)} %get-tuple-element.40, bf16[2,128,384]{2,1,0:T(8,128)(2,1)S(1)} %collective-permute-done.7, bf16[2,128,384]{2,1,0:T(8,128)(2,1)} %collective-permute-done.6, ...), kind=kLoop, calls=%fused_computation.40 | loop fusion | flops 983040 | bytes 2949120 | tf_op jit(solution)/shard_map/convert.1
  69.4 0.7 slice_bitcast_fusion.2
  (44 shorter events, 4.6 us)
Async XLA Ops:
  1.6 19.0 %collective-permute-start.2 = (bf16[2,128,384]{2,1,0:T(8,128)(2,1)S(1)}, bf16[2,128,384]{2,1,0:T(8,128)(2,1)S(1)}, u32[]{:S(2)}, u32[]{:S(2)}) collective-permute-start(bf16[2,128,384]{2,1,0:T(8,128)(2,1)S(1)} %get-tuple-element.23), channel_id=1, source_target_pairs={{64,0},{68,4},{72,8},{76,12},{80,16},{84,20},{88,24},{92,28},{96,3... | collective-permute-start | bytes 589832 | tf_op jit(solution)/shard_map/ppermute | solution.py:14
  2.9 17.6 %collective-permute-start.1 = (bf16[2,128,384]{2,1,0:T(8,128)(2,1)S(1)}, bf16[2,128,384]{2,1,0:T(8,128)(2,1)S(1)}, u32[]{:S(2)}, u32[]{:S(2)}) collective-permute-start(bf16[2,128,384]{2,1,0:T(8,128)(2,1)S(1)} %get-tuple-element.23), channel_id=1, source_target_pairs={{0,64},{4,68},{8,72},{12,76},{16,80},{20,84},{24,88},{28,92},{32,9... | collective-permute-start | bytes 589832 | tf_op jit(solution)/shard_map/ppermute | solution.py:14
  7.8 12.6 %collective-permute-start = (bf16[2,128,384]{2,1,0:T(8,128)(2,1)S(1)}, bf16[2,128,384]{2,1,0:T(8,128)(2,1)S(1)}, u32[]{:S(2)}, u32[]{:S(2)}) collective-permute-start(bf16[2,128,384]{2,1,0:T(8,128)(2,1)S(1)} %get-tuple-element.23), channel_id=1, source_target_pairs={{0,128},{4,132},{8,136},{12,140},{16,144},{20,148},{24,152},{28,15... | collective-permute-start | bytes 589832 | tf_op jit(solution)/shard_map/ppermute | solution.py:14
  13.9 15.2 %collective-permute-start.3 = (bf16[2,128,384]{2,1,0:T(8,128)(2,1)S(1)}, bf16[2,128,384]{2,1,0:T(8,128)(2,1)S(1)}, u32[]{:S(2)}, u32[]{:S(2)}) collective-permute-start(bf16[2,128,384]{2,1,0:T(8,128)(2,1)S(1)} %get-tuple-element.23), channel_id=1, source_target_pairs={{128,0},{132,4},{136,8},{140,12},{144,16},{148,20},{152,24},{156,2... | collective-permute-start | bytes 589832 | tf_op jit(solution)/shard_map/ppermute | solution.py:14
  29.2 0.9 %copy-start = (bf16[128,384]{1,0:T(8,128)(2,1)S(1)}, bf16[128,384]{1,0:T(8,128)(2,1)}, u32[]{:S(2)}) copy-start(bf16[128,384]{1,0:T(8,128)(2,1)} %param.6) | copy-start | bytes 294916
  31.5 0.8 %copy-start.1 = (f32[384]{0:T(512)S(1)}, f32[384]{0:T(512)}, u32[]{:S(2)}) copy-start(f32[384]{0:T(512)} %param.10) | copy-start | bytes 4612
  48.9 14.8 %collective-permute-start.4 = (bf16[2,128,384]{2,1,0:T(8,128)(2,1)}, bf16[2,128,384]{2,1,0:T(8,128)(2,1)S(1)}, u32[]{:S(2)}, u32[]{:S(2)}) collective-permute-start(bf16[2,128,384]{2,1,0:T(8,128)(2,1)} %get-tuple-element.15), channel_id=1, source_target_pairs={{128,0},{132,4},{136,8},{140,12},{144,16},{148,20},{152,24},{156,2... | collective-permute-start | bytes 589832 | tf_op jit(solution)/shard_map/ppermute | solution.py:14
  50.2 13.5 %collective-permute-start.7 = (bf16[2,128,384]{2,1,0:T(8,128)(2,1)}, bf16[2,128,384]{2,1,0:T(8,128)(2,1)S(1)}, u32[]{:S(2)}, u32[]{:S(2)}) collective-permute-start(bf16[2,128,384]{2,1,0:T(8,128)(2,1)} %get-tuple-element.16), channel_id=1, source_target_pairs={{0,128},{4,132},{8,136},{12,140},{16,144},{20,148},{24,152},{28,15... | collective-permute-start | bytes 589832 | tf_op jit(solution)/shard_map/ppermute | solution.py:14
  55.7 8.0 %collective-permute-start.6 = (bf16[2,128,384]{2,1,0:T(8,128)(2,1)S(1)}, bf16[2,128,384]{2,1,0:T(8,128)(2,1)}, u32[]{:S(2)}, u32[]{:S(2)}) collective-permute-start(bf16[2,128,384]{2,1,0:T(8,128)(2,1)S(1)} %get-tuple-element.17), channel_id=1, source_target_pairs={{0,64},{4,68},{8,72},{12,76},{16,80},{20,84},{24,88},{28,92},{32,9... | collective-permute-start | bytes 589832 | tf_op jit(solution)/shard_map/ppermute | solution.py:14
  60.6 7.7 %collective-permute-start.5 = (bf16[2,128,384]{2,1,0:T(8,128)(2,1)S(1)}, bf16[2,128,384]{2,1,0:T(8,128)(2,1)}, u32[]{:S(2)}, u32[]{:S(2)}) collective-permute-start(bf16[2,128,384]{2,1,0:T(8,128)(2,1)S(1)} %get-tuple-element.18), channel_id=1, source_target_pairs={{64,0},{68,4},{72,8},{76,12},{80,16},{84,20},{88,24},{92,28},{96,3... | collective-permute-start | bytes 589832 | tf_op jit(solution)/shard_map/ppermute | solution.py:14
where the time goes:
time: 70.6 us; the launch traced here: 70.1 us
  starting transfers between devices  26.6 us (38%)
  waiting for transfers between devices  13.1 us (19%)
  blocking collectives  12.9 us (18%)
  local copies, waits for them, and re-layouts  6.63 us (9%)
  matrix products  4.15 us (6%)
  between operations  3.56 us (5%)
  other arithmetic  3.26 us (5%)
    ppermute x8, starting transfers between devices, from_behind(): return lax.ppermute(array, axis, pairs)  26.6 us
    ppermute x8, waiting for transfers between devices, from_behind(): return lax.ppermute(array, axis, pairs)  13.1 us
    psum x1, blocking collectives, local(): lax.psum(jnp.sum(attention_wide * attention_wide, axis=1), 'head')  12.9 us
    unnamed x10, local copies, waits for them, and re-layouts  3.4 us
    dot_general x6, matrix products, product(): return jnp.dot(left, right, preferred_element_type=jnp.float32)  1.61 us
  transfers between devices with their start and end apart: 8, of which 2 were waited for; matrix products, arithmetic and copies ran while one was open for 6% of the time, Pallas kernels for 0%

commit v1 on v0

--- a/solution.py
+++ b/solution.py
@@ -73,7 +73,9 @@
         totals.append(total)
     attention = jnp.concatenate(pieces, axis=1)
     attention_wide = attention.astype(jnp.float32)
-    square_sum = lax.psum(jnp.sum(attention_wide * attention_wide, axis=1), "head")
+    square_sum = jnp.sum(
+        lax.all_gather(jnp.sum(attention_wide * attention_wide, axis=1), "head"), axis=0
+    )
     inverse = lax.rsqrt(square_sum / full_width + EPS)
     out = (attention_wide * inverse[:, None] * gain).astype(jnp.bfloat16)
     gradient_pass = d_out.astype(jnp.float32) * gain

time: 70.6 us -> 80.6 us (1.14)
  blocking collectives: 12.9 us -> 22.8 us
    all_gather x0 -> x1, blocking collectives: none -> 9.93 us  [local(): lax.all_gather(jnp.sum(attention_wide * attention_wide, axis=1), 'head')]
where the time goes in v1:
time: 80.6 us; the launch traced here: 80.1 us
  starting transfers between devices  26.6 us (33%)
  blocking collectives  22.8 us (28%)
  waiting for transfers between devices  13.1 us (16%)
  local copies, waits for them, and re-layouts  6.63 us (8%)
  matrix products  4.15 us (5%)
  between operations  3.56 us (4%)
  other arithmetic  3.28 us (4%)
    ppermute x8, starting transfers between devices, from_behind(): return lax.ppermute(array, axis, pairs)  26.6 us
    ppermute x8, waiting for transfers between devices, from_behind(): return lax.ppermute(array, axis, pairs)  13.1 us
    psum x1, blocking collectives, local(): along = lax.psum(jnp.sum(gradient_pass * attention_wide, axis=1), 'head')  12.9 us
    all_gather x1, blocking collectives, local(): lax.all_gather(jnp.sum(attention_wide * attention_wide, axis=1), 'head')  9.93 us
    unnamed x10, local copies, waits for them, and re-layouts  3.4 us
    dot_general x6, matrix products, product(): return jnp.dot(left, right, preferred_element_type=jnp.float32)  1.61 us
  transfers between devices with their start and end apart: 8, of which 2 were waited for; matrix products, arithmetic and copies ran while one was open for 6% of the time, Pallas kernels for 0%

profile of v1, /device:TPU:6, one launch (start us, length us, event | category | flops | bytes accessed | tf_op | source)
XLA Modules:
  0.0 80.1 jit_solution(3968794315789168978)
XLA Ops:
  0.6 1.0 %pad_maximum_fusion.1 = (bf16[2,128,384]{2,1,0:T(8,128)(2,1)S(1)}, bf16[2,640,384]{2,1,0:T(8,128)(2,1)S(1)}) fusion(bf16[1,128,384]{2,1,0:T(8,128)(2,1)} %bitcast.46, bf16[1,128,384]{2,1,0:T(8,128)(2,1)} %bitcast.47), kind=kLoop, calls=%fused_computation.53 | loop fusion | flops 393215 | bytes 589824 | tf_op jit(solution)/shard_map/stack | solution.py:46
  1.6 1.3 %collective-permute-start.2 = (bf16[2,128,384]{2,1,0:T(8,128)(2,1)S(1)}, bf16[2,128,384]{2,1,0:T(8,128)(2,1)S(1)}, u32[]{:S(2)}, u32[]{:S(2)}) collective-permute-start(bf16[2,128,384]{2,1,0:T(8,128)(2,1)S(1)} %get-tuple-element.25), channel_id=1, source_target_pairs={{64,0},{68,4},{72,8},{76,12},{80,16},{84,20},{88,24},{92,28},{96,3... | collective-permute-start | bytes 589832 | tf_op jit(solution)/shard_map/ppermute | solution.py:14
  2.9 4.9 %collective-permute-start.1 = (bf16[2,128,384]{2,1,0:T(8,128)(2,1)S(1)}, bf16[2,128,384]{2,1,0:T(8,128)(2,1)S(1)}, u32[]{:S(2)}, u32[]{:S(2)}) collective-permute-start(bf16[2,128,384]{2,1,0:T(8,128)(2,1)S(1)} %get-tuple-element.25), channel_id=1, source_target_pairs={{0,64},{4,68},{8,72},{12,76},{16,80},{20,84},{24,88},{28,92},{32,9... | collective-permute-start | bytes 589832 | tf_op jit(solution)/shard_map/ppermute | solution.py:14
  7.8 6.1 %collective-permute-start = (bf16[2,128,384]{2,1,0:T(8,128)(2,1)S(1)}, bf16[2,128,384]{2,1,0:T(8,128)(2,1)S(1)}, u32[]{:S(2)}, u32[]{:S(2)}) collective-permute-start(bf16[2,128,384]{2,1,0:T(8,128)(2,1)S(1)} %get-tuple-element.25), channel_id=1, source_target_pairs={{0,128},{4,132},{8,136},{12,140},{16,144},{20,148},{24,152},{28,15... | collective-permute-start | bytes 589832 | tf_op jit(solution)/shard_map/ppermute | solution.py:14
  13.9 1.3 %collective-permute-start.3 = (bf16[2,128,384]{2,1,0:T(8,128)(2,1)S(1)}, bf16[2,128,384]{2,1,0:T(8,128)(2,1)S(1)}, u32[]{:S(2)}, u32[]{:S(2)}) collective-permute-start(bf16[2,128,384]{2,1,0:T(8,128)(2,1)S(1)} %get-tuple-element.25), channel_id=1, source_target_pairs={{128,0},{132,4},{136,8},{140,12},{144,16},{148,20},{152,24},{156,2... | collective-permute-start | bytes 589832 | tf_op jit(solution)/shard_map/ppermute | solution.py:14
  15.2 1.4 %fusion.59 = (s32[1,1]{1,0:T(1,128)}, s32[1,1]{1,0:T(1,128)}, s32[1,1]{1,0:T(1,128)}, s32[1,1]{1,0:T(1,128)}) fusion(s32[1,4]{1,0:T(1,128)} %param.11), kind=kLoop, calls=%fused_computation.108 | loop fusion | bytes 32 | tf_op jit(solution)/shard_map/slice | solution.py:52
  19.5 1.0 %copy.22 = bf16[128,384]{0,1:T(8,128)(2,1)S(1)} copy(bf16[128,384]{1,0:T(8,128)(2,1)} %param.9) | data formatting | bytes 196608 | tf_op args[3]
  20.6 8.5 %collective-permute-done.3 = bf16[2,128,384]{2,1,0:T(8,128)(2,1)S(1)} collective-permute-done((bf16[2,128,384]{2,1,0:T(8,128)(2,1)S(1)}, bf16[2,128,384]{2,1,0:T(8,128)(2,1)S(1)}, u32[]{:S(2)}, u32[]{:S(2)}) %collective-permute-start.3) | collective-permute-done | bytes 196640 | tf_op jit(solution)/shard_map/ppermute | solution.py:14
  29.3 0.8 copy-done
  32.4 12.9 %psum.7 = f32[128]{0:T(128)S(1)} all-reduce(f32[128]{0:T(128)S(1)} %get-tuple-element.15), channel_id=1, replica_groups=mesh['band'=128,'head'=4] {'head'}, use_global_device_ids=true, to_apply=%region_9.10 | all-reduce | flops 128 | bytes 1024 | tf_op jit(solution)/shard_map/psum | solution.py:82
  45.3 9.9 %all-gather.1 = f32[4,1,128]{2,1,0:T(1,128)S(1)} all-gather(f32[1,1,128]{2,1,0:T(1,128)S(1)} %bitcast.48), channel_id=2, replica_groups=mesh['band'=128,'head'=4] {'head'}, dimensions={0}, use_global_device_ids=true | all-gather | bytes 2560 | tf_op jit(solution)/shard_map/all_gather | solution.py:77
  55.6 0.3 fusion.11
  56.3 0.3 fusion.10
  58.0 0.8 %fusion.58 = (bf16[2,128,384]{2,1,0:T(8,128)(2,1)}, bf16[2,128,384]{2,1,0:T(8,128)(2,1)}, bf16[2,128,384]{2,1,0:T(8,128)(2,1)S(1)}, bf16[2,128,384]{2,1,0:T(8,128)(2,1)S(1)}) fusion(bf16[2,640,384]{2,1,0:T(8,128)(2,1)S(1)} %fusion), kind=kLoop, calls=%fused_computation.107 | loop fusion | bytes 1572864 | tf_op jit(solution)/shard_map/slice | solution.py:111
  58.9 1.3 %collective-permute-start.4 = (bf16[2,128,384]{2,1,0:T(8,128)(2,1)}, bf16[2,128,384]{2,1,0:T(8,128)(2,1)S(1)}, u32[]{:S(2)}, u32[]{:S(2)}) collective-permute-start(bf16[2,128,384]{2,1,0:T(8,128)(2,1)} %get-tuple-element.17), channel_id=1, source_target_pairs={{128,0},{132,4},{136,8},{140,12},{144,16},{148,20},{152,24},{156,2... | collective-permute-start | bytes 589832 | tf_op jit(solution)/shard_map/ppermute | solution.py:14
  60.2 5.5 %collective-permute-start.7 = (bf16[2,128,384]{2,1,0:T(8,128)(2,1)}, bf16[2,128,384]{2,1,0:T(8,128)(2,1)S(1)}, u32[]{:S(2)}, u32[]{:S(2)}) collective-permute-start(bf16[2,128,384]{2,1,0:T(8,128)(2,1)} %get-tuple-element.18), channel_id=1, source_target_pairs={{0,128},{4,132},{8,136},{12,140},{16,144},{20,148},{24,152},{28,15... | collective-permute-start | bytes 589832 | tf_op jit(solution)/shard_map/ppermute | solution.py:14
  65.6 5.0 %collective-permute-start.6 = (bf16[2,128,384]{2,1,0:T(8,128)(2,1)S(1)}, bf16[2,128,384]{2,1,0:T(8,128)(2,1)}, u32[]{:S(2)}, u32[]{:S(2)}) collective-permute-start(bf16[2,128,384]{2,1,0:T(8,128)(2,1)S(1)} %get-tuple-element.19), channel_id=1, source_target_pairs={{0,64},{4,68},{8,72},{12,76},{16,80},{20,84},{24,88},{28,92},{32,9... | collective-permute-start | bytes 589832 | tf_op jit(solution)/shard_map/ppermute | solution.py:14
  70.6 1.3 %collective-permute-start.5 = (bf16[2,128,384]{2,1,0:T(8,128)(2,1)S(1)}, bf16[2,128,384]{2,1,0:T(8,128)(2,1)}, u32[]{:S(2)}, u32[]{:S(2)}) collective-permute-start(bf16[2,128,384]{2,1,0:T(8,128)(2,1)S(1)} %get-tuple-element.20), channel_id=1, source_target_pairs={{64,0},{68,4},{72,8},{76,12},{80,16},{84,20},{88,24},{92,28},{96,3... | collective-permute-start | bytes 589832 | tf_op jit(solution)/shard_map/ppermute | solution.py:14
  71.9 0.3 fusion.12
  72.1 0.8 copy.32
  72.9 0.8 copy.33
  73.7 4.6 %collective-permute-done.5 = bf16[2,128,384]{2,1,0:T(8,128)(2,1)} collective-permute-done((bf16[2,128,384]{2,1,0:T(8,128)(2,1)S(1)}, bf16[2,128,384]{2,1,0:T(8,128)(2,1)}, u32[]{:S(2)}, u32[]{:S(2)}) %collective-permute-start.5) | collective-permute-done | bytes 196640 | tf_op jit(solution)/shard_map/ppermute | solution.py:14
  78.2 1.1 %fusion.18 = bf16[2,128,384]{2,1,0:T(8,128)(2,1)S(1)} fusion(f32[1,640,384]{2,1,0:T(8,128)S(1)} %get-tuple-element.41, f32[1,640,384]{2,1,0:T(8,128)S(1)} %get-tuple-element.42, bf16[2,128,384]{2,1,0:T(8,128)(2,1)S(1)} %collective-permute-done.7, bf16[2,128,384]{2,1,0:T(8,128)(2,1)} %collective-permute-done.6, ...), kind=kLoop, calls=%fused_computation.40 | loop fusion | flops 983040 | bytes 2949120 | tf_op jit(solution)/shard_map/convert.1
  79.4 0.7 slice_bitcast_fusion.2
  (46 shorter events, 4.9 us)
Async XLA Ops:
  1.6 19.0 %collective-permute-start.2 = (bf16[2,128,384]{2,1,0:T(8,128)(2,1)S(1)}, bf16[2,128,384]{2,1,0:T(8,128)(2,1)S(1)}, u32[]{:S(2)}, u32[]{:S(2)}) collective-permute-start(bf16[2,128,384]{2,1,0:T(8,128)(2,1)S(1)} %get-tuple-element.25), channel_id=1, source_target_pairs={{64,0},{68,4},{72,8},{76,12},{80,16},{84,20},{88,24},{92,28},{96,3... | collective-permute-start | bytes 589832 | tf_op jit(solution)/shard_map/ppermute | solution.py:14
  2.9 17.6 %collective-permute-start.1 = (bf16[2,128,384]{2,1,0:T(8,128)(2,1)S(1)}, bf16[2,128,384]{2,1,0:T(8,128)(2,1)S(1)}, u32[]{:S(2)}, u32[]{:S(2)}) collective-permute-start(bf16[2,128,384]{2,1,0:T(8,128)(2,1)S(1)} %get-tuple-element.25), channel_id=1, source_target_pairs={{0,64},{4,68},{8,72},{12,76},{16,80},{20,84},{24,88},{28,92},{32,9... | collective-permute-start | bytes 589832 | tf_op jit(solution)/shard_map/ppermute | solution.py:14
  7.8 12.6 %collective-permute-start = (bf16[2,128,384]{2,1,0:T(8,128)(2,1)S(1)}, bf16[2,128,384]{2,1,0:T(8,128)(2,1)S(1)}, u32[]{:S(2)}, u32[]{:S(2)}) collective-permute-start(bf16[2,128,384]{2,1,0:T(8,128)(2,1)S(1)} %get-tuple-element.25), channel_id=1, source_target_pairs={{0,128},{4,132},{8,136},{12,140},{16,144},{20,148},{24,152},{28,15... | collective-permute-start | bytes 589832 | tf_op jit(solution)/shard_map/ppermute | solution.py:14
  13.9 15.2 %collective-permute-start.3 = (bf16[2,128,384]{2,1,0:T(8,128)(2,1)S(1)}, bf16[2,128,384]{2,1,0:T(8,128)(2,1)S(1)}, u32[]{:S(2)}, u32[]{:S(2)}) collective-permute-start(bf16[2,128,384]{2,1,0:T(8,128)(2,1)S(1)} %get-tuple-element.25), channel_id=1, source_target_pairs={{128,0},{132,4},{136,8},{140,12},{144,16},{148,20},{152,24},{156,2... | collective-permute-start | bytes 589832 | tf_op jit(solution)/shard_map/ppermute | solution.py:14
  29.2 0.9 %copy-start = (bf16[128,384]{1,0:T(8,128)(2,1)S(1)}, bf16[128,384]{1,0:T(8,128)(2,1)}, u32[]{:S(2)}) copy-start(bf16[128,384]{1,0:T(8,128)(2,1)} %param.6) | copy-start | bytes 294916
  31.5 0.8 copy-start.1
  58.9 14.8 %collective-permute-start.4 = (bf16[2,128,384]{2,1,0:T(8,128)(2,1)}, bf16[2,128,384]{2,1,0:T(8,128)(2,1)S(1)}, u32[]{:S(2)}, u32[]{:S(2)}) collective-permute-start(bf16[2,128,384]{2,1,0:T(8,128)(2,1)} %get-tuple-element.17), channel_id=1, source_target_pairs={{128,0},{132,4},{136,8},{140,12},{144,16},{148,20},{152,24},{156,2... | collective-permute-start | bytes 589832 | tf_op jit(solution)/shard_map/ppermute | solution.py:14
  60.2 13.5 %collective-permute-start.7 = (bf16[2,128,384]{2,1,0:T(8,128)(2,1)}, bf16[2,128,384]{2,1,0:T(8,128)(2,1)S(1)}, u32[]{:S(2)}, u32[]{:S(2)}) collective-permute-start(bf16[2,128,384]{2,1,0:T(8,128)(2,1)} %get-tuple-element.18), channel_id=1, source_target_pairs={{0,128},{4,132},{8,136},{12,140},{16,144},{20,148},{24,152},{28,15... | collective-permute-start | bytes 589832 | tf_op jit(solution)/shard_map/ppermute | solution.py:14
  65.6 8.0 %collective-permute-start.6 = (bf16[2,128,384]{2,1,0:T(8,128)(2,1)S(1)}, bf16[2,128,384]{2,1,0:T(8,128)(2,1)}, u32[]{:S(2)}, u32[]{:S(2)}) collective-permute-start(bf16[2,128,384]{2,1,0:T(8,128)(2,1)S(1)} %get-tuple-element.19), channel_id=1, source_target_pairs={{0,64},{4,68},{8,72},{12,76},{16,80},{20,84},{24,88},{28,92},{32,9... | collective-permute-start | bytes 589832 | tf_op jit(solution)/shard_map/ppermute | solution.py:14
  70.6 7.7 %collective-permute-start.5 = (bf16[2,128,384]{2,1,0:T(8,128)(2,1)S(1)}, bf16[2,128,384]{2,1,0:T(8,128)(2,1)}, u32[]{:S(2)}, u32[]{:S(2)}) collective-permute-start(bf16[2,128,384]{2,1,0:T(8,128)(2,1)S(1)} %get-tuple-element.20), channel_id=1, source_target_pairs={{64,0},{68,4},{72,8},{76,12},{80,16},{84,20},{88,24},{92,28},{96,3... | collective-permute-start | bytes 589832 | tf_op jit(solution)/shard_map/ppermute | solution.py:14
